TPU v7x, 128 devices: a whole 4x4x4 slice. The times are simulated.
128 devices in a mesh: dp: 16 (over z, x), seq: 8 (over y, core).
Axes of the slice: x: 4, y: 4, z: 4, core: 2. Of those that a mesh axis runs over, the one named last changes fastest.
Arguments:
- hidden: bfloat16 [16, 2, 1024, 5120], P('dp', None, 'seq'), may hold values from -6 to 6
- frozen_queries: bfloat16 [16, 2, 1024, 8192], P('dp', None, 'seq'), may hold values from -120 to 120
- frozen_keys: bfloat16 [16, 2, 1024, 1024], P('dp', None, 'seq'), may hold values from -5 to 5
- frozen_value_matrix: bfloat16 [16, 2, 1024, 1024], P('dp', None, 'seq'), may hold values from -6 to 6
- response_index: int32 [16, 2, 1024], P('dp'), may hold values from 0 to 2, never falling along the last dimension, each value on 1 to 512 neighbouring positions
- partner: int32 [16], P('dp'), may hold values from 0 to 15, as said below
- adapter_down_weight: bfloat16 [5120, 64], replicated, may hold values from -0.078125 to 0.078125
- adapter_up_weight: bfloat16 [64, 1024], replicated, may hold values from -0.75 to 0.75
Outputs:
- attention_out: bfloat16 [16, 2, 1024, 8192], P('dp', None, 'seq')
Inputs may be any that keep to these rules, and one draw needn't show every extreme that they name: partner[r] = r XOR m for one m with 1 <= m < 16, the same for every rank.
All inputs are finite; a program needn't handle non-finite values.
Results may differ from a plain program's by a relative error of at most 0.011.
Values may be sent and summed in bfloat16 or wider, within the bound.
No kernel may reach another device: no remote copies, remote signals or barrier semaphores. Data moves between devices by JAX's collectives and lax.ppermute only.
A program may use at most 128 MiB of HBM per device.

v0:
```python
import jax
import jax.numpy as jnp
from jax import lax
from jax.sharding import PartitionSpec as P

HEAD_SIZE = 128


ADAPTER_SCALE = 2.0


def for_sending(array):
    return jax.tree.map(lambda a: a.astype(jnp.bfloat16) if a.dtype == jnp.float32 else a, array)


def from_partner(block, axis, bit):
    count = lax.axis_size(axis)
    route = []
    for low in range(count):
        high = low | 1 << bit
        if high != low and high < count:
            route += [(low, high), (high, low)]
    return lax.ppermute(block, axis, route)


def attend(queries, key_rows, value_row_block, query_labels, key_labels, query_places, key_places):
    kv_heads = key_rows.shape[1] // HEAD_SIZE
    group_size = queries.shape[1] // (kv_heads * HEAD_SIZE)
    allowed = (query_labels[:, None] == key_labels[None, :]) & (
        key_places[None, :] <= query_places[:, None]
    )

    def one_group(head_group):
        query_block = queries
        query_block = query_block.reshape(queries.shape[0], group_size, HEAD_SIZE)
        scores = jnp.einsum(
            "rgd,cd->rgc", query_block, key_rows, preferred_element_type=jnp.float32
        )
        scores = scores * (1.0 / HEAD_SIZE**0.5)
        scores = jnp.where(allowed[:, None, :], scores, -jnp.inf)
        row_max = jnp.max(scores, axis=2, keepdims=True)
        raised = jnp.exp(scores - row_max)
        weights = (raised / jnp.sum(raised, axis=2, keepdims=True)).astype(jnp.bfloat16)
        blended = jnp.einsum(
            "rgc,cd->rgd", weights, value_row_block, preferred_element_type=jnp.float32
        )
        return blended.astype(jnp.bfloat16)

    blocks = lax.map(one_group, jnp.arange(kv_heads, dtype=jnp.int32))
    return jnp.transpose(blocks, (1, 0, 2, 3)).reshape(queries.shape[0], queries.shape[1])


def apply_value_adapter(hidden_state_rows, frozen_values, adapter_down_weight, adapter_up_weight):
    reduced_state = jnp.dot(
        hidden_state_rows, adapter_down_weight, preferred_element_type=jnp.float32
    ).astype(jnp.bfloat16)
    adapter_delta = jnp.dot(reduced_state, adapter_up_weight, preferred_element_type=jnp.float32)
    return (frozen_values.astype(jnp.float32) + ADAPTER_SCALE * adapter_delta).astype(jnp.bfloat16)


def to_partner(payload, xor_mask):
    bit_count = lax.axis_size("dp").bit_length() - 1
    for bit_number in range(bit_count):
        arrived = jax.tree.map(
            lambda part, own: part.astype(own.dtype),
            from_partner(for_sending(payload), "dp", bit_number),
            payload,
        )
        taking = jnp.bitwise_and(jnp.right_shift(xor_mask, bit_number), 1) == 1
        payload = jax.tree.map(
            lambda came_in, stayed: jnp.where(taking, came_in, stayed), arrived, payload
        )
    return payload


def body(
    hidden,
    frozen_queries,
    frozen_keys,
    frozen_value_matrix,
    response_index,
    partner,
    adapter_down_weight,
    adapter_up_weight,
):
    local_hidden_state = hidden[0]
    own_queries = frozen_queries[0]
    own_keys = frozen_keys[0]
    local_value_rows = frozen_value_matrix[0]
    labels = response_index[0]
    xor_mask = jnp.bitwise_xor(partner[0], lax.axis_index("dp"))
    arrived = to_partner(
        (local_hidden_state[1], own_queries[1], own_keys[1], local_value_rows[1], labels[1]),
        xor_mask,
    )
    local_hidden_state = jnp.stack([local_hidden_state[0], arrived[0]])
    own_queries = jnp.stack([own_queries[0], arrived[1]])
    own_keys = jnp.stack([own_keys[0], arrived[2]])
    local_value_rows = jnp.stack([local_value_rows[0], arrived[3]])
    labels = jnp.stack([labels[0], arrived[4]])
    value_row_block = apply_value_adapter(
        local_hidden_state, local_value_rows, adapter_down_weight, adapter_up_weight
    )
    head_queries, head_keys, head_values = (
        lax.all_to_all(own_queries, "seq", split_axis=2, concat_axis=1, tiled=True),
        lax.all_to_all(own_keys, "seq", split_axis=2, concat_axis=1, tiled=True),
        lax.all_to_all(value_row_block, "seq", split_axis=2, concat_axis=1, tiled=True),
    )
    places = jnp.arange(head_queries.shape[1], dtype=jnp.int32)
    results = jnp.stack(
        [
            attend(
                head_queries[side_index],
                head_keys[side_index],
                head_values[side_index],
                labels[side_index],
                labels[side_index],
                places,
                places,
            )
            for side_index in range(2)
        ]
    )
    results = lax.all_to_all(results, "seq", split_axis=1, concat_axis=2, tiled=True)
    return results[None]


def solution(mesh):
    in_specs = (
        P("dp", None, "seq", None),
        P("dp", None, "seq", None),
        P("dp", None, "seq", None),
        P("dp", None, "seq", None),
        P("dp", None, None),
        P("dp"),
        P(),
        P(),
    )
    out_specs = P("dp", None, "seq", None)
    return jax.shard_map(body, mesh=mesh, in_specs=in_specs, out_specs=out_specs, check_vma=False)
```

profile of v0, /device:TPU:1, one launch (start us, length us, event | category | flops | bytes accessed | tf_op | source)
XLA Modules:
  0.0 588.1 jit_solution(13248085355698181079)
XLA Ops:
  0.0 3.6 slice_bitcast_fusion.3
  8.7 25.2 %collective-permute-done.12 = bf16[128,5120]{1,0:T(8,128)(2,1)} collective-permute-done((bf16[128,5120]{1,0:T(8,128)(2,1)}, bf16[128,5120]{1,0:T(8,128)(2,1)}, u32[]{:S(2)}, u32[]{:S(2)}) %collective-permute-start.12) | collective-permute-done | bytes 1310752 | tf_op jit(solution)/shard_map/ppermute | solution.py:23
  35.2 3.2 collective-permute-start.13
  38.3 40.5 %collective-permute-done = bf16[128,8192]{1,0:T(8,128)(2,1)} collective-permute-done((bf16[128,8192]{1,0:T(8,128)(2,1)}, bf16[128,8192]{1,0:T(8,128)(2,1)}, u32[]{:S(2)}, u32[]{:S(2)}) %collective-permute-start) | collective-permute-done | bytes 2097184 | tf_op jit(solution)/shard_map/ppermute | solution.py:23
  80.7 3.3 collective-permute-start.1
  87.0 70.5 %collective-permute-done.4 = bf16[128,1024]{1,0:T(8,128)(2,1)} collective-permute-done((bf16[128,1024]{1,0:T(8,128)(2,1)}, bf16[128,1024]{1,0:T(8,128)(2,1)}, u32[]{:S(2)}, u32[]{:S(2)}) %collective-permute-start.4) | collective-permute-done | bytes 262176 | tf_op jit(solution)/shard_map/ppermute | solution.py:23
  157.5 3.3 collective-permute-start.5
  164.1 3.3 collective-permute-start.9
  179.3 69.2 %collective-permute-done.6 = bf16[128,1024]{1,0:T(8,128)(2,1)} collective-permute-done((bf16[128,1024]{1,0:T(8,128)(2,1)S(1)}, bf16[128,1024]{1,0:T(8,128)(2,1)}, u32[]{:S(2)}, u32[]{:S(2)}) %collective-permute-start.6) | collective-permute-done | bytes 262176 | tf_op jit(solution)/shard_map/ppermute | solution.py:23
  249.4 3.3 collective-permute-start.7
  255.7 3.2 collective-permute-start.11
  261.6 3.1 broadcast_select_fusion.2
  268.9 12.7 %all-to-all-start.1 = ((bf16[2,128,1024]{1,0,2:T(2,128)(2,1)}), bf16[2,128,1024]{1,0,2:T(2,128)(2,1)S(1)}, u32[]{:S(2)}, u32[]{:S(2)}) async-start(bf16[2,128,1024]{1,0,2:T(2,128)(2,1)} %copy.40), calls=%async_computation.1 | async-start | bytes 1048576 | tf_op jit(solution)/shard_map/all_to_all | solution.py:106
  282.7 13.8 %collective-permute-done.15 = bf16[128,5120]{1,0:T(8,128)(2,1)} collective-permute-done((bf16[128,5120]{1,0:T(8,128)(2,1)}, bf16[128,5120]{1,0:T(8,128)(2,1)}, u32[]{:S(2)}, u32[]{:S(2)}) %collective-permute-start.15) | collective-permute-done | bytes 1310752 | tf_op jit(solution)/shard_map/ppermute | solution.py:23
  303.0 38.5 %collective-permute-done.3 = bf16[128,8192]{1,0:T(8,128)(2,1)} collective-permute-done((bf16[128,8192]{1,0:T(8,128)(2,1)}, bf16[128,8192]{1,0:T(8,128)(2,1)}, u32[]{:S(2)}, u32[]{:S(2)}) %collective-permute-start.3) | collective-permute-done | bytes 2097184 | tf_op jit(solution)/shard_map/ppermute | solution.py:23
  343.3 8.4 %all-to-all-start.2 = ((bf16[2,128,1024]{1,0,2:T(2,128)(2,1)}), bf16[2,128,1024]{1,0,2:T(2,128)(2,1)S(1)}, u32[]{:S(2)}, u32[]{:S(2)}) async-start(bf16[2,128,1024]{1,0,2:T(2,128)(2,1)} %copy.43), calls=%async_computation.2 | async-start | bytes 1048576 | tf_op jit(solution)/shard_map/all_to_all | solution.py:107
  351.7 4.0 pad_maximum_fusion
  355.6 11.1 %copy.38 = bf16[2,128,8192]{1,0,2:T(2,128)(2,1)} copy(bf16[2,128,8192]{2,1,0:T(8,128)(2,1)} %pad_maximum_fusion) | data formatting | bytes 8388608 | tf_op jit(solution)/shard_map/stack | solution.py:97
  366.8 4.9 all-to-all-start
  374.9 3.8 collective-permute-done.17
  388.6 32.0 %all-to-all-done = bf16[2,128,8192]{1,0,2:T(2,128)(2,1)} async-done(((bf16[2,128,8192]{1,0,2:T(2,128)(2,1)}), bf16[2,128,8192]{1,0,2:T(2,128)(2,1)}, u32[]{:S(2)}, u32[]{:S(2)}) %all-to-all-start) | async-done | bytes 4194336 | tf_op jit(solution)/shard_map/all_to_all | solution.py:105
  420.6 11.1 %copy.39 = bf16[2,128,8,1024]{3,1,2,0:T(8,128)(2,1)} copy(bf16[2,128,8,1024]{1,0,3,2:T(2,128)(2,1)} %bitcast.5) | data formatting | bytes 8388608 | tf_op jit(solution)/shard_map/all_to_all | solution.py:105
  437.0 18.8 %fusion.60 = (f32[1024,8]{0,1:T(8,128)S(1)}, f32[1024,8,1024]{0,2,1:T(8,128)}) fusion(pred[1024,1024]{0,1:T(8,128)(4,1)} %fusion.12, bf16[1024,128,1]{1,0,2:T(8,128)(2,1)S(1)} %bitcast.101, bf16[1024,8,128]{2,1,0:T(8,128)(2,1)S(1)} %bitcast.95), kind=kOutput, calls=%fused_computation.81 | convolution fusion | flops 2181039104 | bytes 36995072 | tf_op jit(solution)/shard_map/while/body/eval_jaxpr/sub | solution.py:42
  455.8 11.8 %fusion.22 = bf16[1024,8,128]{0,2,1:T(8,128)(2,1)S(1)} fusion(bf16[1024,128,1]{0,1,2:T(8,128)(2,1)S(1)} %reshape.113, f32[1024,8,1024]{0,2,1:T(8,128)} %get-tuple-element.58, f32[1024,8]{0,1:T(8,128)S(1)} %get-tuple-element.57), kind=kOutput, calls=%fused_computation.35 | convolution fusion | flops 2165309440 | bytes 35946496 | tf_op jit(solution)/shard_map/while/body/eval_jaxpr/rgc,cd->rgd/dot_general | solution.py:44
  467.7 7.5 %copy.49 = bf16[1,1024,1024]{2,0,1:T(2,128)(2,1)} copy(bf16[1,1024,1024]{1,2,0:T(8,128)(2,1)S(1)} %bitcast.92) | data formatting | bytes 4194304 | tf_op jit(solution)/shard_map/stack;reshape;transpose | solution.py:110
  475.2 19.0 %fusion.65 = (f32[1024,8]{0,1:T(8,128)S(1)}, f32[1024,8,1024]{0,2,1:T(8,128)}) fusion(pred[1024,1024]{0,1:T(8,128)(4,1)} %fusion.13, bf16[1024,128,1]{1,0,2:T(8,128)(2,1)S(1)} %bitcast.100, bf16[1024,8,128]{2,1,0:T(8,128)(2,1)} %bitcast.94), kind=kOutput, calls=%fused_computation.82 | convolution fusion | flops 2181039104 | bytes 36995072 | tf_op jit(solution)/shard_map/while/body/eval_jaxpr/sub | solution.py:42
  494.2 11.9 %fusion.23 = bf16[1024,8,128]{0,2,1:T(8,128)(2,1)S(1)} fusion(bf16[1024,128,1]{0,1,2:T(8,128)(2,1)S(1)} %reshape.111, f32[1024,8,1024]{0,2,1:T(8,128)} %get-tuple-element.60, f32[1024,8]{0,1:T(8,128)S(1)} %get-tuple-element.59), kind=kOutput, calls=%fused_computation.36 | convolution fusion | flops 2165309440 | bytes 35946496 | tf_op jit(solution)/shard_map/while/body/eval_jaxpr/rgc,cd->rgd/dot_general | solution.py:44
  506.1 7.7 %copy.48 = bf16[1,1024,1024]{2,0,1:T(2,128)(2,1)} copy(bf16[1,1024,1024]{1,2,0:T(8,128)(2,1)S(1)} %bitcast.93) | data formatting | bytes 4194304 | tf_op jit(solution)/shard_map/stack;reshape;transpose | solution.py:110
  513.8 10.0 %pad_maximum_fusion.1 = bf16[2,1024,1024]{2,0,1:T(2,128)(2,1)S(1)} fusion(bf16[1,1024,1024]{2,0,1:T(2,128)(2,1)} %copy.49, bf16[1,1024,1024]{2,0,1:T(2,128)(2,1)} %copy.48), kind=kLoop, calls=%fused_computation.19 | loop fusion | flops 8388608 | bytes 8388608 | tf_op jit(solution)/shard_map/stack | solution.py:110
  523.8 52.6 %all_to_all.60 = bf16[2,1024,1024]{2,0,1:T(2,128)(2,1)S(1)} all-to-all(bf16[2,1024,1024]{2,0,1:T(2,128)(2,1)S(1)} %pad_maximum_fusion.1), channel_id=1, replica_groups=mesh['dp'=16,'seq'=8] {'seq'}, dimensions={1} | all-to-all | bytes 8388608 | tf_op jit(solution)/shard_map/all_to_all | solution.py:124
  576.5 4.3 copy.50
  580.8 7.4 %broadcast_in_dim.53 = bf16[1,2,128,8192]{3,2,1,0:T(8,128)(2,1)} reshape(bf16[2,128,8,1024]{3,2,1,0:T(8,128)(2,1)} %copy.50) | data formatting | bytes 8388608 | tf_op jit(solution)/shard_map/broadcast_in_dim | solution.py:125
  (87 shorter events, 64.2 us)
Async XLA Ops:
  0.0 299.1 %copy-start = (bf16[5120,64]{0,1:T(8,128)(2,1)S(1)}, bf16[5120,64]{0,1:T(8,128)(2,1)}, u32[]{:S(2)}) copy-start(bf16[5120,64]{0,1:T(8,128)(2,1)} %param.14) | copy-start | bytes 1966084
  0.0 5.6 copy-start.2
  3.6 30.4 %copy-start.4 = (bf16[1,2,128,5120]{3,2,1,0:T(8,128)(2,1)S(1)}, bf16[1,2,128,5120]{3,2,1,0:T(8,128)(2,1)}, u32[]{:S(2)}) copy-start(bf16[1,2,128,5120]{3,2,1,0:T(8,128)(2,1)} %param.8) | copy-start | bytes 7864324
  3.6 30.3 %collective-permute-start.12 = (bf16[128,5120]{1,0:T(8,128)(2,1)}, bf16[128,5120]{1,0:T(8,128)(2,1)}, u32[]{:S(2)}, u32[]{:S(2)}) collective-permute-start(bf16[128,5120]{1,0:T(8,128)(2,1)} %get-tuple-element.38), channel_id=1, source_target_pairs={{0,8},{8,0},{16,24},{24,16},{32,40},{40,32},{48,56},{56,48},{64,72... | collective-permute-start | bytes 3932168 | tf_op jit(solution)/shard_map/ppermute | solution.py:23
  8.1 70.8 %collective-permute-start = (bf16[128,8192]{1,0:T(8,128)(2,1)}, bf16[128,8192]{1,0:T(8,128)(2,1)}, u32[]{:S(2)}, u32[]{:S(2)}) collective-permute-start(bf16[128,8192]{1,0:T(8,128)(2,1)} %get-tuple-element.36), channel_id=1, source_target_pairs={{0,8},{8,0},{16,24},{24,16},{32,40},{40,32},{48,56},{56,48},{64,72... | collective-permute-start | bytes 6291464 | tf_op jit(solution)/shard_map/ppermute | solution.py:23
  35.2 48.8 %copy-start.6 = (bf16[1,2,128,1024]{3,2,1,0:T(8,128)(2,1)S(1)}, bf16[1,2,128,1024]{3,2,1,0:T(8,128)(2,1)}, u32[]{:S(2)}) copy-start(bf16[1,2,128,1024]{3,2,1,0:T(8,128)(2,1)} %param.10) | copy-start | bytes 1572868
  35.2 49.9 %copy-start.7 = (bf16[1,2,128,1024]{3,2,1,0:T(8,128)(2,1)S(1)}, bf16[1,2,128,1024]{3,2,1,0:T(8,128)(2,1)}, u32[]{:S(2)}) copy-start(bf16[1,2,128,1024]{3,2,1,0:T(8,128)(2,1)} %param.11) | copy-start | bytes 1572868
  35.2 132.2 %collective-permute-start.13 = (bf16[128,5120]{1,0:T(8,128)(2,1)}, bf16[128,5120]{1,0:T(8,128)(2,1)}, u32[]{:S(2)}, u32[]{:S(2)}) collective-permute-start(bf16[128,5120]{1,0:T(8,128)(2,1)} %broadcast_select_fusion.3), channel_id=1, source_target_pairs={{0,16},{16,0},{8,24},{24,8},{32,48},{48,32},{40,56},{56,40},{64,80... | collective-permute-start | bytes 3932168 | tf_op jit(solution)/shard_map/ppermute | solution.py:23
  80.7 89.3 %copy-start.3 = (bf16[128,8192]{1,0:T(8,128)(2,1)}, bf16[128,8192]{1,0:T(8,128)(2,1)S(1)}, u32[]{:S(2)}) copy-start(bf16[128,8192]{1,0:T(8,128)(2,1)S(1)} %broadcast_select_fusion) | copy-start | bytes 6291460
  80.7 90.9 %collective-permute-start.1 = (bf16[128,8192]{1,0:T(8,128)(2,1)S(1)}, bf16[128,8192]{1,0:T(8,128)(2,1)}, u32[]{:S(2)}, u32[]{:S(2)}) collective-permute-start(bf16[128,8192]{1,0:T(8,128)(2,1)S(1)} %broadcast_select_fusion), channel_id=1, source_target_pairs={{0,16},{16,0},{8,24},{24,8},{32,48},{48,32},{40,56},{56,40},{64,80... | collective-permute-start | bytes 6291464 | tf_op jit(solution)/shard_map/ppermute | solution.py:23
  84.7 72.8 %collective-permute-start.4 = (bf16[128,1024]{1,0:T(8,128)(2,1)}, bf16[128,1024]{1,0:T(8,128)(2,1)}, u32[]{:S(2)}, u32[]{:S(2)}) collective-permute-start(bf16[128,1024]{1,0:T(8,128)(2,1)} %get-tuple-element.52), channel_id=1, source_target_pairs={{0,8},{8,0},{16,24},{24,16},{32,40},{40,32},{48,56},{56,48},{64,72... | collective-permute-start | bytes 786440 | tf_op jit(solution)/shard_map/ppermute | solution.py:23
  85.9 77.2 %collective-permute-start.8 = (bf16[128,1024]{1,0:T(8,128)(2,1)}, bf16[128,1024]{1,0:T(8,128)(2,1)}, u32[]{:S(2)}, u32[]{:S(2)}) collective-permute-start(bf16[128,1024]{1,0:T(8,128)(2,1)} %get-tuple-element.54), channel_id=1, source_target_pairs={{0,8},{8,0},{16,24},{24,16},{32,40},{40,32},{48,56},{56,48},{64,72... | collective-permute-start | bytes 786440 | tf_op jit(solution)/shard_map/ppermute | solution.py:23
  157.5 15.9 %collective-permute-start.5 = (bf16[128,1024]{1,0:T(8,128)(2,1)S(1)}, bf16[128,1024]{1,0:T(8,128)(2,1)S(1)}, u32[]{:S(2)}, u32[]{:S(2)}) collective-permute-start(bf16[128,1024]{1,0:T(8,128)(2,1)S(1)} %broadcast_select_fusion.7), channel_id=1, source_target_pairs={{0,16},{16,0},{8,24},{24,8},{32,48},{48,32},{40,56},{56,40},{64,80... | collective-permute-start | bytes 786440 | tf_op jit(solution)/shard_map/ppermute | solution.py:23
  164.1 12.8 %collective-permute-start.9 = (bf16[128,1024]{1,0:T(8,128)(2,1)S(1)}, bf16[128,1024]{1,0:T(8,128)(2,1)S(1)}, u32[]{:S(2)}, u32[]{:S(2)}) collective-permute-start(bf16[128,1024]{1,0:T(8,128)(2,1)S(1)} %broadcast_select_fusion.6), channel_id=1, source_target_pairs={{0,16},{16,0},{8,24},{24,8},{32,48},{48,32},{40,56},{56,40},{64,80... | collective-permute-start | bytes 786440 | tf_op jit(solution)/shard_map/ppermute | solution.py:23
  169.9 89.1 %collective-permute-start.14 = (bf16[128,5120]{1,0:T(8,128)(2,1)}, bf16[128,5120]{1,0:T(8,128)(2,1)}, u32[]{:S(2)}, u32[]{:S(2)}) collective-permute-start(bf16[128,5120]{1,0:T(8,128)(2,1)} %broadcast_select_fusion.4), channel_id=1, source_target_pairs={{0,32},{32,0},{8,40},{40,8},{16,48},{48,16},{24,56},{56,24},{64,96... | collective-permute-start | bytes 3932168 | tf_op jit(solution)/shard_map/ppermute | solution.py:23
  173.4 88.2 %collective-permute-start.2 = (bf16[128,8192]{1,0:T(8,128)(2,1)S(1)}, bf16[128,8192]{1,0:T(8,128)(2,1)}, u32[]{:S(2)}, u32[]{:S(2)}) collective-permute-start(bf16[128,8192]{1,0:T(8,128)(2,1)S(1)} %broadcast_select_fusion.1), channel_id=1, source_target_pairs={{0,32},{32,0},{8,40},{40,8},{16,48},{48,16},{24,56},{56,24},{64,96... | collective-permute-start | bytes 6291464 | tf_op jit(solution)/shard_map/ppermute | solution.py:23
  173.5 74.9 %collective-permute-start.6 = (bf16[128,1024]{1,0:T(8,128)(2,1)S(1)}, bf16[128,1024]{1,0:T(8,128)(2,1)}, u32[]{:S(2)}, u32[]{:S(2)}) collective-permute-start(bf16[128,1024]{1,0:T(8,128)(2,1)S(1)} %broadcast_select_fusion.9), channel_id=1, source_target_pairs={{0,32},{32,0},{8,40},{40,8},{16,48},{48,16},{24,56},{56,24},{64,96... | collective-permute-start | bytes 786440 | tf_op jit(solution)/shard_map/ppermute | solution.py:23
  177.6 76.5 %collective-permute-start.10 = (bf16[128,1024]{1,0:T(8,128)(2,1)}, bf16[128,1024]{1,0:T(8,128)(2,1)}, u32[]{:S(2)}, u32[]{:S(2)}) collective-permute-start(bf16[128,1024]{1,0:T(8,128)(2,1)} %broadcast_select_fusion.8), channel_id=1, source_target_pairs={{0,32},{32,0},{8,40},{40,8},{16,48},{48,16},{24,56},{56,24},{64,96... | collective-permute-start | bytes 786440 | tf_op jit(solution)/shard_map/ppermute | solution.py:23
  249.4 18.2 %collective-permute-start.7 = (bf16[128,1024]{1,0:T(8,128)(2,1)S(1)}, bf16[128,1024]{1,0:T(8,128)(2,1)S(1)}, u32[]{:S(2)}, u32[]{:S(2)}) collective-permute-start(bf16[128,1024]{1,0:T(8,128)(2,1)S(1)} %broadcast_select_fusion.11), channel_id=1, source_target_pairs={{0,64},{64,0},{8,72},{72,8},{16,80},{80,16},{24,88},{88,24},{32,96... | collective-permute-start | bytes 786440 | tf_op jit(solution)/shard_map/ppermute | solution.py:23
  255.7 25.8 %collective-permute-start.11 = (bf16[128,1024]{1,0:T(8,128)(2,1)}, bf16[128,1024]{1,0:T(8,128)(2,1)}, u32[]{:S(2)}, u32[]{:S(2)}) collective-permute-start(bf16[128,1024]{1,0:T(8,128)(2,1)} %broadcast_select_fusion.10), channel_id=1, source_target_pairs={{0,64},{64,0},{8,72},{72,8},{16,80},{80,16},{24,88},{88,24},{32,96... | collective-permute-start | bytes 786440 | tf_op jit(solution)/shard_map/ppermute | solution.py:23
  261.6 35.0 %collective-permute-start.15 = (bf16[128,5120]{1,0:T(8,128)(2,1)}, bf16[128,5120]{1,0:T(8,128)(2,1)}, u32[]{:S(2)}, u32[]{:S(2)}) collective-permute-start(bf16[128,5120]{1,0:T(8,128)(2,1)} %broadcast_select_fusion.5), channel_id=1, source_target_pairs={{0,64},{64,0},{8,72},{72,8},{16,80},{80,16},{24,88},{88,24},{32,96... | collective-permute-start | bytes 3932168 | tf_op jit(solution)/shard_map/ppermute | solution.py:23
  264.7 76.8 %collective-permute-start.3 = (bf16[128,8192]{1,0:T(8,128)(2,1)}, bf16[128,8192]{1,0:T(8,128)(2,1)}, u32[]{:S(2)}, u32[]{:S(2)}) collective-permute-start(bf16[128,8192]{1,0:T(8,128)(2,1)} %broadcast_select_fusion.2), channel_id=1, source_target_pairs={{0,64},{64,0},{8,72},{72,8},{16,80},{80,16},{24,88},{88,24},{32,96... | collective-permute-start | bytes 6291464 | tf_op jit(solution)/shard_map/ppermute | solution.py:23
  268.9 74.4 %all-to-all-start.1 = ((bf16[2,128,1024]{1,0,2:T(2,128)(2,1)}), bf16[2,128,1024]{1,0,2:T(2,128)(2,1)S(1)}, u32[]{:S(2)}, u32[]{:S(2)}) async-start(bf16[2,128,1024]{1,0,2:T(2,128)(2,1)} %copy.40), calls=%async_computation.1 | async-start | bytes 1048576 | tf_op jit(solution)/shard_map/all_to_all | solution.py:106
  281.6 17.5 %copy-start.5 = (bf16[1,128,5120]{2,1,0:T(8,128)(2,1)S(1)}, bf16[1,128,5120]{2,1,0:T(8,128)(2,1)}, u32[]{:S(2)}) copy-start(bf16[1,128,5120]{2,1,0:T(8,128)(2,1)} %get-tuple-element.37) | copy-start | bytes 3932164
  281.6 17.5 %copy-start.8 = (bf16[1,128,1024]{2,1,0:T(8,128)(2,1)S(1)}, bf16[1,128,1024]{2,1,0:T(8,128)(2,1)}, u32[]{:S(2)}) copy-start(bf16[1,128,1024]{2,1,0:T(8,128)(2,1)} %get-tuple-element.53) | copy-start | bytes 786436
  343.3 23.5 %all-to-all-start.2 = ((bf16[2,128,1024]{1,0,2:T(2,128)(2,1)}), bf16[2,128,1024]{1,0,2:T(2,128)(2,1)S(1)}, u32[]{:S(2)}, u32[]{:S(2)}) async-start(bf16[2,128,1024]{1,0,2:T(2,128)(2,1)} %copy.43), calls=%async_computation.2 | async-start | bytes 1048576 | tf_op jit(solution)/shard_map/all_to_all | solution.py:107
  366.8 53.8 %all-to-all-start = ((bf16[2,128,8192]{1,0,2:T(2,128)(2,1)}), bf16[2,128,8192]{1,0,2:T(2,128)(2,1)}, u32[]{:S(2)}, u32[]{:S(2)}) async-start(bf16[2,128,8192]{1,0,2:T(2,128)(2,1)} %copy.38), calls=%async_computation | async-start | bytes 8388608 | tf_op jit(solution)/shard_map/all_to_all | solution.py:105
  371.7 2.5 collective-permute-start.16
  374.3 4.4 collective-permute-start.17
  378.7 2.9 collective-permute-start.18
  381.5 4.4 collective-permute-start.19
  576.5 11.7 %copy-start.1 = (bf16[5120,64]{0,1:T(8,128)(2,1)S(1)}, bf16[5120,64]{0,1:T(8,128)(2,1)}, u32[]{:S(2)}) copy-start(bf16[5120,64]{0,1:T(8,128)(2,1)} %param.14) | copy-start | bytes 1966084
  (1 other events, 4.9 us)
where the time goes:
time: 590 us; the launch traced here: 588 us
  waiting for transfers between devices  307 us (52%)
  local copies, waits for them, and re-layouts  65.4 us (11%)
  matrix products  64.3 us (11%)
  starting transfers between devices  57.9 us (10%)
  blocking collectives  52.6 us (9%)
  other arithmetic  40.2 us (7%)
    ppermute x20, waiting for transfers between devices, from_partner(): return lax.ppermute(block, axis, route)  275 us
    all_to_all x1, blocking collectives, body(): lax.all_to_all(results, 'seq', split_axis=1, concat_axis=2, tiled=True)  52.6 us
    sub x2, matrix products, one_group(): raised = jnp.exp(scores - row_max)  37.8 us
    all_to_all x1, waiting for transfers between devices, body(): lax.all_to_all(own_queries, 'seq', split_axis=2, concat_axis=1, tiled=True)  32 us
    ppermute x20, starting transfers between devices, from_partner(): return lax.ppermute(block, axis, route)  31.9 us
    dot_general x2, matrix products, one_group(): jnp.einsum('rgc,cd->rgd', weights, value_row_block, preferred_element_typ...  23.7 us
    select_n x16, other arithmetic, to_partner(): jnp.where(taking, came_in, stayed)  17.5 us
    another operation x2, local copies, waits for them, and re-layouts, body(): jnp.stack([attend(head_queries[side_index], head_keys[side_index], head_v...  15.3 us
  transfers between devices with their start and end apart: 23, of which 14 were waited for; matrix products, arithmetic and copies ran while one was open for 9% of the time, Pallas kernels for 0%

commit v1 on v0

v1 whole, which is shorter than its diff:
```python
import functools

import jax
import jax.numpy as jnp
from jax import lax
from jax.experimental import pallas as pl
from jax.experimental.pallas import tpu as pltpu
from jax.sharding import PartitionSpec as P

HEAD = 128
GROUP = 8
KV = 8
ROWS = 128
SPAN = GROUP * HEAD
PAIR = 2
ADAPTER_SCALE = 2.0
EXP2_SCALE = 1.4426950408889634 / HEAD**0.5
MASKED = -jnp.inf
VMEM_LIMIT = 60 << 20

KEPT = 4
MOVED = KV - KEPT
LABELS_AT = MOVED * 2 * HEAD


def fill_bias(bias_ref, own_at, places, label_at):
    def label_row(at):
        found = jnp.where(at >= 0, label_at(jnp.maximum(at, 0)).astype(jnp.float32), -1.0)
        return jnp.broadcast_to(found, (ROWS, ROWS))

    mine = label_row(own_at)
    query_label = mine.T
    merged = jnp.where(causal(), mine, label_row(own_at - 4))
    for at, tile in enumerate([merged] + [label_row(place) for place in places]):
        bias_ref[at] = jnp.where(tile == query_label, 0.0, MASKED)


def other_places(own_at):
    low_core = lax.rem(own_at, 2) == 0
    return own_at - 2, jnp.where(low_core, own_at - 1, own_at - 3), jnp.where(low_core, own_at - 3, own_at - 1)


def causal():
    rows = lax.broadcasted_iota(jnp.int32, (ROWS, ROWS), 0)
    return lax.broadcasted_iota(jnp.int32, (ROWS, ROWS), 1) <= rows


def adapter_kernel(
    place_ref, labels_ref, hidden_ref, down_ref, frozen_ref, key_ref, up_ref, query_ref,
    near_ref, moved_ref, moved_query_ref, bias_zero_ref, bias_one_ref, low_ref, sem,
):
    step = pl.program_id(0)
    copy = pltpu.make_async_copy(query_ref.at[0, 1, :, pl.ds(KEPT * SPAN, MOVED * SPAN)], moved_query_ref, sem)

    @pl.when(step == 0)
    def _():
        copy.start()
        low_ref[...] = jnp.zeros_like(low_ref)
        own_at = place_ref[0]
        for half, bias_ref in enumerate((bias_zero_ref, bias_one_ref)):
            label_at = lambda at: labels_ref[half : half + 1, pl.ds(pl.multiple_of(at * ROWS, ROWS), ROWS)]
            fill_bias(bias_ref, own_at, other_places(own_at), label_at)

    low_ref[...] += lax.dot_general(
        hidden_ref[...].reshape(2 * ROWS, hidden_ref.shape[-1]),
        down_ref[...],
        (((1,), (1,)), ((), ())),
        preferred_element_type=jnp.float32,
    )

    @pl.when(step == pl.num_programs(0) - 1)
    def _():
        low = low_ref[...].astype(jnp.bfloat16)
        delta = jnp.dot(low, up_ref[...], preferred_element_type=jnp.float32)
        for half in range(2):
            own = delta[half * ROWS : (half + 1) * ROWS]
            values = (frozen_ref[half].astype(jnp.float32) + ADAPTER_SCALE * own).astype(jnp.bfloat16)
            for head in range(KV):
                if half == 0:
                    out, at = near_ref, KEPT + head
                else:
                    out, at = (near_ref, head) if head < KEPT else (moved_ref, head - KEPT)
                cols = slice(head * HEAD, (head + 1) * HEAD)
                out[:, 2 * at * HEAD : (2 * at + 1) * HEAD] = key_ref[half, :, cols]
                out[:, (2 * at + 1) * HEAD : (2 * at + 2) * HEAD] = values[:, cols]
        labels = [labels_ref[1:2, at * ROWS : (at + 1) * ROWS].astype(jnp.float32) for at in range(8)]
        labels = jnp.concatenate(labels + [jnp.zeros((ROWS - 8, HEAD), jnp.float32)], axis=0)
        moved_ref[:, LABELS_AT:] = labels.astype(jnp.bfloat16)
        copy.wait()


def adapter(place, labels, hidden, frozen_values, keys, down, up, queries):
    width = hidden.shape[-1]
    steps = 4
    part = width // steps
    rank = down.shape[0]
    shapes = [
        ((ROWS, (KEPT + KV) * 2 * HEAD), jnp.bfloat16),
        ((ROWS, LABELS_AT + HEAD), jnp.bfloat16),
        ((ROWS, MOVED * SPAN), jnp.bfloat16),
        ((4, ROWS, ROWS), jnp.float32),
        ((4, ROWS, ROWS), jnp.float32),
    ]
    return pl.pallas_call(
        adapter_kernel,
        grid_spec=pltpu.PrefetchScalarGridSpec(
            num_scalar_prefetch=1,
            grid=(steps,),
            in_specs=[
                pl.BlockSpec((None, 2, 8 * ROWS), lambda i, p: (0, 0, 0)),
                pl.BlockSpec((None, 2, ROWS, part), lambda i, p: (0, 0, 0, i)),
                pl.BlockSpec((rank, part), lambda i, p: (0, i)),
                pl.BlockSpec((None, 2, ROWS, KV * HEAD), lambda i, p: (0, 0, 0, 0)),
                pl.BlockSpec((None, 2, ROWS, KV * HEAD), lambda i, p: (0, 0, 0, 0)),
                pl.BlockSpec((rank, KV * HEAD), lambda i, p: (0, 0)),
                pl.BlockSpec(memory_space=pl.ANY),
            ],
            out_specs=[
                pl.BlockSpec(memory_space=pl.ANY) if at == 2 else pl.BlockSpec(shape, lambda i, p, n=len(shape): (0,) * n)
                for at, (shape, _) in enumerate(shapes)
            ],
            scratch_shapes=[pltpu.VMEM((2 * ROWS, rank), jnp.float32), pltpu.SemaphoreType.DMA],
        ),
        out_shape=[jax.ShapeDtypeStruct(*shape) for shape in shapes],
        compiler_params=pltpu.CompilerParams(vmem_limit_bytes=60 << 20),
        cost_estimate=pl.CostEstimate(flops=1 << 20, bytes_accessed=1 << 20, transcendentals=0),
        name="adapter",
    )(place, labels, hidden, down, frozen_values, keys, up, queries)


def near_attention_kernel(unroll, bias_ref, query_ref, own_ref, far_ref, two_ref, x_ref, w_ref, out_ref, key_ref, value_ref):
    blocks = (own_ref, far_ref, two_ref, x_ref, w_ref)
    attend(unroll, bias_ref, query_ref, blocks, out_ref, key_ref, value_ref)


def moved_attention_kernel(
    unroll, place_ref, label_ref, query_ref, own_ref, far_ref, two_ref, x_ref, w_ref, _,
    out_ref, bias_ref, key_ref, value_ref,
):
    @pl.when(pl.program_id(0) == 0)
    def _():
        own_at = place_ref[0]
        rows = label_ref[...].astype(jnp.float32)
        chosen = lax.broadcasted_iota(jnp.int32, rows.shape, 0)

        def label_at(at):
            return jnp.sum(jnp.where(chosen == at, rows, 0.0), axis=0, keepdims=True)

        fill_bias(bias_ref, own_at, other_places(own_at), label_at)

    blocks = (own_ref, far_ref, two_ref, x_ref, w_ref)
    attend(unroll, bias_ref, query_ref, blocks, out_ref, key_ref, value_ref)


def attend(unroll, bias_ref, query_ref, blocks, out_ref, key_ref, value_ref):
    is_causal = causal()

    @pl.when(pl.program_id(0) == 0)
    def _():
        value_ref[:, HEAD:] = jnp.ones((5 * ROWS, HEAD), jnp.bfloat16)

    for at, block in enumerate(blocks):
        span = slice(at * ROWS, (at + 1) * ROWS)
        key_ref[span, :] = block[:, :HEAD]
        value_ref[span, :HEAD] = block[:, HEAD:]

    def some_heads(step, carry):
        spans = [pl.ds(pl.multiple_of((step * PAIR + i) * HEAD, HEAD), HEAD) for i in range(PAIR)]
        queries = jnp.concatenate([query_ref[:, span] for span in spans], axis=0)
        scores = lax.dot_general(
            queries, key_ref[...], (((1,), (1,)), ((), ())), preferred_element_type=jnp.float32
        )
        weights = []
        for i in range(PAIR):
            mine = scores[i * ROWS : (i + 1) * ROWS]
            tiles = [jnp.where(is_causal, mine[:, :ROWS], mine[:, ROWS : 2 * ROWS]) + bias_ref[0]]
            tiles += [mine[:, (t + 1) * ROWS : (t + 2) * ROWS] + bias_ref[t] for t in range(1, 4)]
            peak = jnp.maximum(jnp.maximum(tiles[0], tiles[1]), jnp.maximum(tiles[2], tiles[3]))
            peak = jnp.max(peak, axis=1, keepdims=True)
            raised = [jnp.exp2((tile - peak) * EXP2_SCALE) for tile in tiles]
            near = jnp.where(is_causal, raised[0], 0.0).astype(jnp.bfloat16)
            far = jnp.where(is_causal, 0.0, raised[0]).astype(jnp.bfloat16)
            weights.append(
                jnp.concatenate([near, far] + [r.astype(jnp.bfloat16) for r in raised[1:]], axis=1)
            )
        blended = jnp.dot(
            jnp.concatenate(weights, axis=0), value_ref[...], preferred_element_type=jnp.float32
        )
        result = (blended[:, :HEAD] / blended[:, HEAD:]).astype(jnp.bfloat16)
        for i, span in enumerate(spans):
            out_ref[:, span] = result[i * ROWS : (i + 1) * ROWS]
        return carry

    steps = GROUP // PAIR
    if unroll == steps:
        for step in range(steps):
            some_heads(step, 0)
    else:
        lax.fori_loop(0, steps, some_heads, 0, unroll=unroll)


SCRATCH = [pltpu.VMEM((5 * ROWS, HEAD), jnp.bfloat16), pltpu.VMEM((5 * ROWS, 2 * HEAD), jnp.bfloat16)]
OUT = jax.ShapeDtypeStruct((1, 2, ROWS, KV * SPAN), jnp.bfloat16)


def near_attention(unroll, half, count, first, bias, queries, blocks, out_shape, out_spec):
    own, far, two, pair = blocks
    block_spec = pl.BlockSpec((ROWS, 2 * HEAD), lambda i: (0, first + i))
    return pl.pallas_call(
        functools.partial(near_attention_kernel, unroll),
        grid=(count,),
        in_specs=[
            pl.BlockSpec((4, ROWS, ROWS), lambda i: (0, 0, 0)),
            pl.BlockSpec((None, None, ROWS, SPAN), lambda i: (0, half, 0, i)),
        ]
        + [block_spec] * 3
        + [pl.BlockSpec((ROWS, 2 * HEAD), lambda i, row=row: (row, i)) for row in range(2)],
        out_specs=out_spec,
        scratch_shapes=SCRATCH,
        out_shape=out_shape,
        compiler_params=pltpu.CompilerParams(vmem_limit_bytes=VMEM_LIMIT),
        cost_estimate=pl.CostEstimate(flops=1 << 20, bytes_accessed=1 << 20, transcendentals=0),
        name="near_attention",
    )(bias, queries, own, far, two, pair, pair)


def moved_attention(place, queries, blocks, into):
    own, far, two, pair = blocks
    block_spec = pl.BlockSpec((ROWS, 2 * HEAD), lambda i, p: (0, i))
    return pl.pallas_call(
        functools.partial(moved_attention_kernel, 4),
        grid_spec=pltpu.PrefetchScalarGridSpec(
            num_scalar_prefetch=1,
            grid=(MOVED,),
            in_specs=[
                pl.BlockSpec((16, HEAD), lambda i, p: (0, LABELS_AT // HEAD)),
                pl.BlockSpec((ROWS, SPAN), lambda i, p: (0, i)),
            ]
            + [block_spec] * 3
            + [pl.BlockSpec((ROWS, 2 * HEAD), lambda i, p, row=row: (row, i)) for row in range(2)]
            + [pl.BlockSpec(memory_space=pl.ANY)],
            out_specs=pl.BlockSpec((None, None, ROWS, SPAN), lambda i, p: (0, 1, 0, KEPT + i)),
            scratch_shapes=[pltpu.VMEM((4, ROWS, ROWS), jnp.float32)] + SCRATCH,
        ),
        out_shape=OUT,
        input_output_aliases={8: 0},
        compiler_params=pltpu.CompilerParams(vmem_limit_bytes=VMEM_LIMIT),
        cost_estimate=pl.CostEstimate(flops=1 << 20, bytes_accessed=1 << 20, transcendentals=0),
        name="moved_attention",
    )(place, own, queries, own, far, two, pair, pair, into)


def shift(block, step):
    return lax.ppermute(block, "seq", [(s, s + step) for s in range(8 - step)])


def other_core(block):
    return lax.ppermute(block, "seq", [(s, s ^ 1) for s in range(8)])


def exchange(block, far, two, low_core, cols):
    pair = jnp.concatenate([two[:, cols], jnp.where(low_core, block[:, cols], far[:, cols])], axis=0)
    return block, far, two, other_core(pair)


def body(hidden, queries, keys, frozen_values, labels, partner, down, up):
    place = lax.axis_index("seq").astype(jnp.int32)
    low_core = lax.rem(place, 2) == 0
    place = place.reshape((1,))
    mask = jnp.bitwise_xor(partner[0], lax.axis_index("dp"))
    near, kv_moved, moved_queries, bias_zero, bias_one = adapter(
        place, labels, hidden, frozen_values, keys, down.T, up, queries
    )
    near_two, near_far = shift(near, 2), shift(near, 4)

    def route(m):
        return [(r, r ^ m) for r in range(16)]

    def move(m, kv_moved, moved_queries):
        return lax.ppermute(kv_moved, "dp", route(m)), lax.ppermute(moved_queries, "dp", route(m))

    kv_moved, moved_queries = lax.switch(
        mask - 1, [functools.partial(move, m) for m in range(1, 16)], kv_moved, moved_queries
    )
    kv_moved, moved_queries, near_two, near_far = lax.optimization_barrier(
        (kv_moved, moved_queries, near_two, near_far)
    )
    split = KEPT * 2 * HEAD
    kept_blocks = exchange(near, near_far, near_two, low_core, slice(0, split))
    zero_blocks = exchange(near, near_far, near_two, low_core, slice(split, None))
    sent = near_attention(
        4, 1, KEPT, 0, bias_one, queries, kept_blocks,
        jax.ShapeDtypeStruct((ROWS, KEPT * SPAN), jnp.bfloat16), pl.BlockSpec((ROWS, SPAN), lambda i: (0, i)),
    )

    def send(m, sent, kv_moved, bias, queries, *blocks):
        came = lax.ppermute(sent, "dp", route(m))
        two, far = shift(kv_moved, 2), shift(kv_moved, 4)
        spec = pl.BlockSpec((None, None, ROWS, SPAN), lambda i: (0, 0, 0, i))
        return came, two, far, near_attention(2, 0, KV, KEPT, bias, queries, blocks, OUT, spec)

    came, two, far, out = lax.switch(
        mask - 1, [functools.partial(send, m) for m in range(1, 16)], sent, kv_moved, bias_zero, queries, *zero_blocks
    )
    moved_blocks = exchange(kv_moved, far, two, low_core, slice(0, LABELS_AT))
    out = lax.dynamic_update_slice(out, came[None, None], (0, 1, 0, 0))
    return moved_attention(place, moved_queries, moved_blocks, out)


def solution(mesh):
    in_specs = (
        P("dp", None, "seq", None),
        P("dp", None, "seq", None),
        P("dp", None, "seq", None),
        P("dp", None, "seq", None),
        P("dp", None, None),
        P("dp"),
        P(),
        P(),
    )
    out_specs = P("dp", None, "seq", None)
    return jax.shard_map(body, mesh=mesh, in_specs=in_specs, out_specs=out_specs, check_vma=False)
```

time: 590 us -> 105 us (0.18)
  waiting for transfers between devices: 307 us -> 33.9 us
  matrix products: 64.3 us -> 0 us
  local copies, waits for them, and re-layouts: 65.4 us -> 5.87 us
  blocking collectives: 52.6 us -> 0 us
  other arithmetic: 40.2 us -> 2.22 us
  Pallas kernels: 0 us -> 36.7 us
  starting transfers between devices: 57.9 us -> 27 us
    ppermute x20 -> x10, waiting for transfers between devices: 275 us -> 33.9 us  [the longest x1 28.6 us: move(): lax.ppermute(kv_moved, 'dp', route(m))]
    all_to_all x1 -> x0, blocking collectives: 52.6 us -> none  [body(): lax.all_to_all(results, 'seq', split_axis=1, concat_axis=2, tiled=True)]
    sub x2 -> x0, matrix products: 37.8 us -> none  [one_group(): raised = jnp.exp(scores - row_max)]
    pallas_call x0 -> x4, Pallas kernels: none -> 36.7 us  [the longest x2 23.6 us: near_attention(): pl.pallas_call(functools.partial(near_attention_kernel, unroll), grid=(co...]
    all_to_all x3 -> x0, waiting for transfers between devices: 32 us -> none  [the longest x1 32 us: body(): lax.all_to_all(own_queries, 'seq', split_axis=2, concat_axis=1, tiled=True)]
    another operation x4 -> x0, local copies, waits for them, and re-layouts: 27.5 us -> none  [the longest x2 15.3 us: body(): jnp.stack([attend(head_queries[side_index], head_keys[side_index], head_v...]
    dot_general x3 -> x0, matrix products: 26.5 us -> none  [the longest x2 23.7 us: one_group(): jnp.einsum('rgc,cd->rgd', weights, value_row_block, preferred_element_typ...]
    all_to_all x3 -> x0, starting transfers between devices: 26 us -> none  [the longest x1 12.7 us: body(): lax.all_to_all(own_keys, 'seq', split_axis=2, concat_axis=1, tiled=True)]
  transfers between devices with their start and end apart: 23 -> 10, of which waited for: 14 -> 4; matrix products, arithmetic and copies ran while one was open for 9% -> 2% of each run, Pallas kernels for 0% -> 22%
where the time goes in v1:
time: 105 us; the launch traced here: 107 us
  Pallas kernels  36.7 us (35%)
  waiting for transfers between devices  33.9 us (32%)
  starting transfers between devices  27 us (26%)
  local copies, waits for them, and re-layouts  5.87 us (6%)
  other arithmetic  2.22 us (2%)
    ppermute x1, waiting for transfers between devices, move(): lax.ppermute(kv_moved, 'dp', route(m))  28.6 us
    pallas_call x2, Pallas kernels, near_attention(): pl.pallas_call(functools.partial(near_attention_kernel, unroll), grid=(co...  23.6 us
    ppermute x4, starting transfers between devices, shift(): return lax.ppermute(block, 'seq', [(s, s + step) for s in range(8 - step)])  12.6 us
    pallas_call x1, Pallas kernels, moved_attention(): pl.pallas_call(functools.partial(moved_attention_kernel, 4), grid_spec=pl...  7.94 us
    ppermute x1, starting transfers between devices, move(): lax.ppermute(moved_queries, 'dp', route(m))  5.9 us
    ppermute x1, starting transfers between devices, send(): came = lax.ppermute(sent, 'dp', route(m))  5.15 us
    pallas_call x1, Pallas kernels, adapter(): pl.pallas_call(adapter_kernel, grid_spec=pltpu.PrefetchScalarGridSpec(num...  5.15 us
    ppermute x3, waiting for transfers between devices, other_core(): return lax.ppermute(block, 'seq', [(s, s ^ 1) for s in range(8)])  4.38 us
  transfers between devices with their start and end apart: 10, of which 4 were waited for; matrix products, arithmetic and copies ran while one was open for 2% of the time, Pallas kernels for 22%

profile of v1, /device:TPU:1, one launch (start us, length us, event | category | flops | bytes accessed | tf_op | source)
XLA Modules:
  0.0 106.8 jit_solution(7392193052596734215)
XLA Ops:
  0.0 5.1 %adapter.1 = (bf16[128,3072]{1,0:T(8,128)(2,1)S(1)}, bf16[128,1152]{1,0:T(8,128)(2,1)}, bf16[128,4096]{1,0:T(8,128)(2,1)S(1)}, f32[4,128,128]{2,1,0:T(8,128)}, f32[4,128,128]{2,1,0:T(8,128)}) custom-call(s32[1]{0:T(128)} %bitcast.15.place_ref, s32[1,2,1024]{2,1,0:T(2,128)} %labels_ref.1, bf16[1,2,128,5120]{3,2,1,0:T(8,128)(2,1)} %hidden_ref.1, ...), custom_call_target="tpu_custom_call" | custom-call | flops 1048576 | bytes 1048576 | tf_op jit(solution)/shard_map/adapter/pallas_call | solution.py:104
  5.2 5.7 %collective-permute-start.76 = (bf16[128,3072]{1,0:T(8,128)(2,1)S(1)}, bf16[128,3072]{1,0:T(8,128)(2,1)S(1)}, u32[]{:S(2)}, u32[]{:S(2)}) collective-permute-start(bf16[128,3072]{1,0:T(8,128)(2,1)S(1)} %get-tuple-element.479.own_ref), channel_id=1, source_target_pairs={{0,4},{1,5},{2,6},{3,7},{8,12},{9,13},{10,14},{11,15},{16,20},{17,... | collective-permute-start | bytes 2359304 | tf_op jit(solution)/shard_map/ppermute | solution.py:254
  10.8 2.4 %collective-permute-start.75 = (bf16[128,3072]{1,0:T(8,128)(2,1)S(1)}, bf16[128,3072]{1,0:T(8,128)(2,1)S(1)}, u32[]{:S(2)}, u32[]{:S(2)}) collective-permute-start(bf16[128,3072]{1,0:T(8,128)(2,1)S(1)} %get-tuple-element.479.own_ref), channel_id=1, source_target_pairs={{0,2},{1,3},{2,4},{3,5},{4,6},{5,7},{8,10},{9,11},{10,12},{11,13},... | collective-permute-start | bytes 2359304 | tf_op jit(solution)/shard_map/ppermute | solution.py:254
  13.8 34.6 %conditional.2 = (bf16[128,1152]{1,0:T(8,128)(2,1)}, bf16[128,4096]{1,0:T(8,128)(2,1)}) conditional(s32[]{:T(128)} %clamp.4, (bf16[128,1152]{1,0:T(8,128)(2,1)}, bf16[128,4096]{1,0:T(8,128)(2,1)S(1)}) %tuple.186, (bf16[128,1152]{1,0:T(8,128)(2,1)}, bf16[128,4096]{1,0:T(8,128)(2,1)S(1)}) %tuple.186, ...), branch_computations={%region_0.0_spmd, %region_1.0_spmd, %region_2.0_spmd, %region_3.0_... | conditional | bytes 5374048 | solution.py:282
  13.9 5.9 %collective-permute-start.21 = (bf16[128,4096]{1,0:T(8,128)(2,1)S(1)}, bf16[128,4096]{1,0:T(8,128)(2,1)}, u32[]{:S(2)}, u32[]{:S(2)}) collective-permute-start(bf16[128,4096]{1,0:T(8,128)(2,1)S(1)} %get-tuple-element.330), channel_id=1, source_target_pairs={{0,88},{8,80},{16,72},{24,64},{32,120},{40,112},{48,104},{56,96},{... | collective-permute-start | bytes 3145736 | tf_op jit(solution)/shard_map/cond/branch_10_fun/ppermute | solution.py:280
  19.8 0.1 collective-permute-start.20
  19.9 28.6 %collective-permute-done.20 = bf16[128,1152]{1,0:T(8,128)(2,1)} collective-permute-done((bf16[128,1152]{1,0:T(8,128)(2,1)}, bf16[128,1152]{1,0:T(8,128)(2,1)}, u32[]{:S(2)}, u32[]{:S(2)}) %collective-permute-start.20) | collective-permute-done | bytes 294944 | tf_op jit(solution)/shard_map/cond/branch_10_fun/ppermute | solution.py:280
  48.5 0.0 collective-permute-done.21
  48.5 0.0 collective-permute-done.76.far_ref
  48.5 0.1 slice_select_fusion
  48.6 1.1 %pad_maximum_fusion = bf16[256,2048]{1,0:T(8,128)(2,1)} fusion(bf16[128,2048]{1,0:T(8,128)(2,1)S(1)} %slice_select_fusion, bf16[128,2048]{1,0:T(8,128)(2,1)S(1)} %slice.116), kind=kLoop, calls=%fused_computation.15 | loop fusion | flops 2097152 | bytes 2097152 | tf_op jit(solution)/shard_map/concatenate | solution.py:262
  49.7 1.9 %collective-permute-start.78 = (bf16[256,2048]{1,0:T(8,128)(2,1)}, bf16[256,2048]{1,0:T(8,128)(2,1)S(1)}, u32[]{:S(2)}, u32[]{:S(2)}) collective-permute-start(bf16[256,2048]{1,0:T(8,128)(2,1)} %pad_maximum_fusion), channel_id=1, source_target_pairs={{0,1},{1,0},{2,3},{3,2},{4,5},{5,4},{6,7},{7,6},{8,9},{9,8},{10,11... | collective-permute-start | bytes 3145736 | tf_op jit(solution)/shard_map/ppermute | solution.py:258
  51.6 0.1 collective-permute-start.77
  51.7 2.8 %collective-permute-done.77.x_ref.w_ref = bf16[256,1024]{1,0:T(8,128)(2,1)S(1)} collective-permute-done((bf16[256,1024]{1,0:T(8,128)(2,1)S(1)}, bf16[256,1024]{1,0:T(8,128)(2,1)S(1)}, u32[]{:S(2)}, u32[]{:S(2)}) %collective-permute-start.77) | collective-permute-done | bytes 524320 | tf_op jit(solution)/shard_map/ppermute | solution.py:258
  54.6 0.8 copy-done.2
  55.4 7.9 %near_attention.31 = bf16[128,4096]{1,0:T(8,128)(2,1)} custom-call(f32[4,128,128]{2,1,0:T(8,128)} %get-tuple-element.482.bias_ref, bf16[1,2,128,8192]{3,2,1,0:T(8,128)(2,1)} %query_ref.3, bf16[128,3072]{1,0:T(8,128)(2,1)S(1)} %get-tuple-element.479.own_ref, bf16[128,3072]{1,0:T(8,128)(2,1)S(1)} %collective-permute-done.76.far_ref, ...), custom_call_target="tpu_custom_call" | custom-call | flops 1048576 | bytes 1048576 | tf_op jit(solution)/shard_map/near_attention/pallas_call | solution.py:209
  63.2 0.0 collective-permute-done.78
  63.2 31.0 %conditional.3 = (bf16[128,1152]{1,0:T(8,128)(2,1)}, bf16[128,1152]{1,0:T(8,128)(2,1)}, bf16[1,1,128,4096]{3,2,1,0:T(8,128)(2,1)}, bf16[128,1024]{1,0:T(8,128)(2...) conditional(s32[]{:T(128)} %clamp.4, ...), branch_computations={%region_15.16_spmd, %region_16.17_spmd, %region_17.18_spmd, %regio... | conditional | flops 1048576 | bytes 10748072 | solution.py:302
  63.6 5.2 %collective-permute-start.62 = (bf16[128,4096]{1,0:T(8,128)(2,1)}, bf16[128,4096]{1,0:T(8,128)(2,1)}, u32[]{:S(2)}, u32[]{:S(2)}) collective-permute-start(bf16[128,4096]{1,0:T(8,128)(2,1)} %get-tuple-element.420), channel_id=1, source_target_pairs={{0,88},{8,80},{16,72},{24,64},{32,120},{40,112},{48,104},{56,96},{... | collective-permute-start | bytes 3145736 | tf_op jit(solution)/shard_map/cond/branch_10_fun/ppermute | solution.py:297
  68.7 2.5 %collective-permute-start.61 = (bf16[128,1152]{1,0:T(8,128)(2,1)}, bf16[128,1152]{1,0:T(8,128)(2,1)}, u32[]{:S(2)}, u32[]{:S(2)}) collective-permute-start(bf16[128,1152]{1,0:T(8,128)(2,1)} %get-tuple-element.419), channel_id=1, source_target_pairs={{0,4},{1,5},{2,6},{3,7},{8,12},{9,13},{10,14},{11,15},{16,20},{17,... | collective-permute-start | bytes 884744 | tf_op jit(solution)/shard_map/cond/branch_10_fun/ppermute | solution.py:254
  71.2 2.1 %collective-permute-start.60 = (bf16[128,1152]{1,0:T(8,128)(2,1)}, bf16[128,1152]{1,0:T(8,128)(2,1)}, u32[]{:S(2)}, u32[]{:S(2)}) collective-permute-start(bf16[128,1152]{1,0:T(8,128)(2,1)} %get-tuple-element.419), channel_id=1, source_target_pairs={{0,2},{1,3},{2,4},{3,5},{4,6},{5,7},{8,10},{9,11},{10,12},{11,13},... | collective-permute-start | bytes 884744 | tf_op jit(solution)/shard_map/cond/branch_10_fun/ppermute | solution.py:254
  73.3 15.7 %near_attention.26 = bf16[1,2,128,8192]{3,2,1,0:T(8,128)(2,1)} custom-call(f32[4,128,128]{2,1,0:T(8,128)S(1)} %get-tuple-element.421.bias_ref, bf16[1,2,128,8192]{3,2,1,0:T(8,128)(2,1)} %get-tuple-element.422.query_ref, bf16[128,3072]{1,0:T(8,128)(2,1)S(1)} %get-tuple-element.423.own_ref, bf16[128,3072]{1,0:T(8,128)(2,1)S(1)} %get-tuple-element.424.far_ref, ...), custom_call_target="tpu_custom_call" | custom-call | flops 1048576 | bytes 1048576 | tf_op jit(solution)/shard_map/cond/branch_10_fun/near_attention/pallas_call | solution.py:209
  89.0 0.0 collective-permute-done.61
  89.0 1.0 slice.141
  90.0 1.0 slice.140
  91.0 0.9 collective-permute-done.62
  91.9 2.3 %constant_dynamic-update-slice_fusion.10 = bf16[1,2,128,8192]{3,2,1,0:T(8,128)(2,1)} fusion(bf16[1,2,128,8192]{3,2,1,0:T(8,128)(2,1)} %near_attention.26, bf16[128,4096]{1,0:T(8,128)(2,1)} %collective-permute-done.62), kind=kLoop, calls=%fused_computation.10 | loop fusion | bytes 2097152 | tf_op jit(solution)/shard_map/dynamic_update_slice | solution.py:306
  94.2 1.0 slice_select_fusion.1
  95.3 1.3 %collective-permute-start.79 = (bf16[256,1024]{1,0:T(8,128)(2,1)S(1)}, bf16[256,1024]{1,0:T(8,128)(2,1)S(1)}, u32[]{:S(2)}, u32[]{:S(2)}) collective-permute-start(bf16[256,1024]{1,0:T(8,128)(2,1)S(1)} %pad_maximum_fusion.2), channel_id=1, source_target_pairs={{0,1},{1,0},{2,3},{3,2},{4,5},{5,4},{6,7},{7,6},{8,9},{9,8},{10,11... | collective-permute-start | bytes 1572872 | tf_op jit(solution)/shard_map/ppermute | solution.py:258
  96.5 1.5 %collective-permute-done.79.x_ref.w_ref = bf16[256,1024]{1,0:T(8,128)(2,1)S(1)} collective-permute-done((bf16[256,1024]{1,0:T(8,128)(2,1)S(1)}, bf16[256,1024]{1,0:T(8,128)(2,1)S(1)}, u32[]{:S(2)}, u32[]{:S(2)}) %collective-permute-start.79) | collective-permute-done | bytes 524320 | tf_op jit(solution)/shard_map/ppermute | solution.py:258
  98.1 0.8 copy-done.1
  98.9 7.9 %moved_attention.1 = bf16[1,2,128,8192]{3,2,1,0:T(8,128)(2,1)} custom-call(s32[1]{0:T(128)} %bitcast.15.place_ref, bf16[128,1152]{1,0:T(8,128)(2,1)} %get-tuple-element.480.label_ref.own_ref, bf16[128,4096]{1,0:T(8,128)(2,1)} %get-tuple-element.481.query_ref, bf16[128,1152]{1,0:T(8,128)(2,1)} %get-tuple-element.480.label_ref.own_ref, ...), custom_call_target="tpu_custom_call", output_to_operand_aliasing={{}: (8, {})} | custom-call | flops 1048576 | bytes 1048576 | tf_op jit(solution)/shard_map/moved_attention/pallas_call | solution.py:230
  (11 shorter events, 0.2 us)
Async XLA Ops:
  5.2 43.3 %collective-permute-start.76 = (bf16[128,3072]{1,0:T(8,128)(2,1)S(1)}, bf16[128,3072]{1,0:T(8,128)(2,1)S(1)}, u32[]{:S(2)}, u32[]{:S(2)}) collective-permute-start(bf16[128,3072]{1,0:T(8,128)(2,1)S(1)} %get-tuple-element.479.own_ref), channel_id=1, source_target_pairs={{0,4},{1,5},{2,6},{3,7},{8,12},{9,13},{10,14},{11,15},{16,20},{17,... | collective-permute-start | bytes 2359304 | tf_op jit(solution)/shard_map/ppermute | solution.py:254
  10.8 37.6 %collective-permute-start.75 = (bf16[128,3072]{1,0:T(8,128)(2,1)S(1)}, bf16[128,3072]{1,0:T(8,128)(2,1)S(1)}, u32[]{:S(2)}, u32[]{:S(2)}) collective-permute-start(bf16[128,3072]{1,0:T(8,128)(2,1)S(1)} %get-tuple-element.479.own_ref), channel_id=1, source_target_pairs={{0,2},{1,3},{2,4},{3,5},{4,6},{5,7},{8,10},{9,11},{10,12},{11,13},... | collective-permute-start | bytes 2359304 | tf_op jit(solution)/shard_map/ppermute | solution.py:254
  13.9 34.6 %collective-permute-start.21 = (bf16[128,4096]{1,0:T(8,128)(2,1)S(1)}, bf16[128,4096]{1,0:T(8,128)(2,1)}, u32[]{:S(2)}, u32[]{:S(2)}) collective-permute-start(bf16[128,4096]{1,0:T(8,128)(2,1)S(1)} %get-tuple-element.330), channel_id=1, source_target_pairs={{0,88},{8,80},{16,72},{24,64},{32,120},{40,112},{48,104},{56,96},{... | collective-permute-start | bytes 3145736 | tf_op jit(solution)/shard_map/cond/branch_10_fun/ppermute | solution.py:280
  19.8 28.7 %collective-permute-start.20 = (bf16[128,1152]{1,0:T(8,128)(2,1)}, bf16[128,1152]{1,0:T(8,128)(2,1)}, u32[]{:S(2)}, u32[]{:S(2)}) collective-permute-start(bf16[128,1152]{1,0:T(8,128)(2,1)} %get-tuple-element.329), channel_id=1, source_target_pairs={{0,88},{8,80},{16,72},{24,64},{32,120},{40,112},{48,104},{56,96},{... | collective-permute-start | bytes 884744 | tf_op jit(solution)/shard_map/cond/branch_10_fun/ppermute | solution.py:280
  49.7 13.6 %collective-permute-start.78 = (bf16[256,2048]{1,0:T(8,128)(2,1)}, bf16[256,2048]{1,0:T(8,128)(2,1)S(1)}, u32[]{:S(2)}, u32[]{:S(2)}) collective-permute-start(bf16[256,2048]{1,0:T(8,128)(2,1)} %pad_maximum_fusion), channel_id=1, source_target_pairs={{0,1},{1,0},{2,3},{3,2},{4,5},{5,4},{6,7},{7,6},{8,9},{9,8},{10,11... | collective-permute-start | bytes 3145736 | tf_op jit(solution)/shard_map/ppermute | solution.py:258
  51.6 2.9 %collective-permute-start.77 = (bf16[256,1024]{1,0:T(8,128)(2,1)S(1)}, bf16[256,1024]{1,0:T(8,128)(2,1)S(1)}, u32[]{:S(2)}, u32[]{:S(2)}) collective-permute-start(bf16[256,1024]{1,0:T(8,128)(2,1)S(1)} %pad_maximum_fusion.1), channel_id=1, source_target_pairs={{0,1},{1,0},{2,3},{3,2},{4,5},{5,4},{6,7},{7,6},{8,9},{9,8},{10,11... | collective-permute-start | bytes 1572872 | tf_op jit(solution)/shard_map/ppermute | solution.py:258
  54.6 0.8 copy-start.2
  55.4 7.9 %copy-start = (f32[4,128,128]{2,1,0:T(8,128)S(1)}, f32[4,128,128]{2,1,0:T(8,128)}, u32[]{:S(2)}) copy-start(f32[4,128,128]{2,1,0:T(8,128)} %get-tuple-element.485) | copy-start | bytes 786436
  63.6 28.4 %collective-permute-start.62 = (bf16[128,4096]{1,0:T(8,128)(2,1)}, bf16[128,4096]{1,0:T(8,128)(2,1)}, u32[]{:S(2)}, u32[]{:S(2)}) collective-permute-start(bf16[128,4096]{1,0:T(8,128)(2,1)} %get-tuple-element.420), channel_id=1, source_target_pairs={{0,88},{8,80},{16,72},{24,64},{32,120},{40,112},{48,104},{56,96},{... | collective-permute-start | bytes 3145736 | tf_op jit(solution)/shard_map/cond/branch_10_fun/ppermute | solution.py:297
  68.7 20.3 %collective-permute-start.61 = (bf16[128,1152]{1,0:T(8,128)(2,1)}, bf16[128,1152]{1,0:T(8,128)(2,1)}, u32[]{:S(2)}, u32[]{:S(2)}) collective-permute-start(bf16[128,1152]{1,0:T(8,128)(2,1)} %get-tuple-element.419), channel_id=1, source_target_pairs={{0,4},{1,5},{2,6},{3,7},{8,12},{9,13},{10,14},{11,15},{16,20},{17,... | collective-permute-start | bytes 884744 | tf_op jit(solution)/shard_map/cond/branch_10_fun/ppermute | solution.py:254
  71.2 18.8 %collective-permute-start.60 = (bf16[128,1152]{1,0:T(8,128)(2,1)}, bf16[128,1152]{1,0:T(8,128)(2,1)}, u32[]{:S(2)}, u32[]{:S(2)}) collective-permute-start(bf16[128,1152]{1,0:T(8,128)(2,1)} %get-tuple-element.419), channel_id=1, source_target_pairs={{0,2},{1,3},{2,4},{3,5},{4,6},{5,7},{8,10},{9,11},{10,12},{11,13},... | collective-permute-start | bytes 884744 | tf_op jit(solution)/shard_map/cond/branch_10_fun/ppermute | solution.py:254
  95.3 2.8 %collective-permute-start.79 = (bf16[256,1024]{1,0:T(8,128)(2,1)S(1)}, bf16[256,1024]{1,0:T(8,128)(2,1)S(1)}, u32[]{:S(2)}, u32[]{:S(2)}) collective-permute-start(bf16[256,1024]{1,0:T(8,128)(2,1)S(1)} %pad_maximum_fusion.2), channel_id=1, source_target_pairs={{0,1},{1,0},{2,3},{3,2},{4,5},{5,4},{6,7},{7,6},{8,9},{9,8},{10,11... | collective-permute-start | bytes 1572872 | tf_op jit(solution)/shard_map/ppermute | solution.py:258
  98.1 0.8 copy-start.1
